TPU v7x, 256 devices: a whole 4x4x8 slice. The times are simulated.
256 devices in a mesh: dp: 32 (over x_hi, z, core), fsdp: 8 (over x_lo, y).
Axes of the slice: x: 4 (x_hi: 2, x_lo: 2; x = x_hi * 2 + x_lo), y: 4, z: 8, core: 2. Of those that a mesh axis runs over, the one named last changes fastest.
Arguments:
- states: bfloat16 [49152, 5120], P(('dp', 'fsdp')), may hold values from -24 to 24
- steps: int32 [256], P(('dp', 'fsdp')), may hold values from 0 to 999
- frozen_query_rows: bfloat16 [49152, 5120], P(('dp', 'fsdp')), may hold values from -6 to 6
- frozen_key_rows: bfloat16 [49152, 5120], P(('dp', 'fsdp')), may hold values from -18 to 18
- frozen_value_rows: bfloat16 [49152, 5120], P(('dp', 'fsdp')), may hold values from -6 to 6
- cotangent: bfloat16 [49152, 5120], P(('dp', 'fsdp')), may hold values from -24 to 24
- adapter_down_maps: bfloat16 [2, 5120, 128], P(None, 'fsdp'), may hold values from -0.078125 to 0.078125
- adapter_up_maps: bfloat16 [2, 128, 5120], P(None, None, 'fsdp'), may hold values from -0.5 to 0.5
Outputs:
- grad_down: float32 [2, 5120, 128], P(None, 'fsdp')
- grad_up: float32 [2, 128, 5120], P(None, None, 'fsdp')
All inputs are finite; a program needn't handle non-finite values.
Results may differ from a plain program's by a relative error of at most 0.012.
Values may be sent and summed in bfloat16 or wider, within the bound.
No kernel may reach another device: no remote copies, remote signals or barrier semaphores. Data moves between devices by JAX's collectives and lax.ppermute only.
A program may use at most 128 MiB of HBM per device.

v0:
```python
import math
import jax
import jax.numpy as jnp
from jax import lax
from jax.sharding import PartitionSpec as P

HEADS = 40
NSTEPS = 1000


def rounded(value):
    return lax.optimization_barrier(value.astype(jnp.bfloat16)).astype(jnp.float32)


def clip_objective(
    down_matrix,
    up_matrix,
    states,
    frozen_query_rows,
    frozen_key_rows,
    frozen_value_rows,
    cotangent,
    weight,
):
    highest = lax.Precision.HIGHEST
    length = states.shape[0]
    width = states.shape[1]
    head_size = width // HEADS
    inputs = states.astype(jnp.float32)
    center = inputs - jnp.mean(inputs, axis=1, keepdims=True)
    spread = jnp.mean(center * center, axis=1, keepdims=True)
    normed = rounded(center * lax.rsqrt(spread + 1e-06))
    low = rounded(jnp.einsum("td,jdr->jtr", normed, down_matrix, precision=highest))
    delta = jnp.einsum("jtr,jrd->jtd", low, up_matrix, precision=highest)
    query = rounded(frozen_query_rows.astype(jnp.float32) + delta[0]).reshape(
        length, HEADS, head_size
    )
    value = rounded(frozen_value_rows.astype(jnp.float32) + delta[1]).reshape(
        length, HEADS, head_size
    )
    keys = frozen_key_rows.astype(jnp.float32).reshape(length, HEADS, head_size)
    scores = jnp.einsum("qhe,khe->hqk", query, keys, precision=highest) * (
        1.0 / math.sqrt(head_size)
    )
    probs = rounded(jax.nn.softmax(scores, axis=-1))
    attended = jnp.einsum("hqk,khe->qhe", probs, value, precision=highest).reshape(length, width)
    return weight * jnp.sum(attended * cotangent.astype(jnp.float32))


def local(
    states,
    steps,
    frozen_query_rows,
    frozen_key_rows,
    frozen_value_rows,
    cotangent,
    adapter_down_maps,
    adapter_up_maps,
):
    down_matrix, up_matrix = (
        lax.all_gather(adapter_down_maps, "fsdp", axis=1, tiled=True),
        lax.all_gather(adapter_up_maps, "fsdp", axis=2, tiled=True),
    )
    weight = (steps[0].astype(jnp.float32) + 1.0) / NSTEPS
    grad_fn = jax.grad(clip_objective, argnums=(0, 1))
    local_down, local_up = grad_fn(
        down_matrix.astype(jnp.float32),
        up_matrix.astype(jnp.float32),
        states,
        frozen_query_rows,
        frozen_key_rows,
        frozen_value_rows,
        cotangent,
        weight,
    )
    data_count = lax.axis_size("dp")
    group_count = lax.axis_size("fsdp")
    width = local_down.shape[1]
    rank_size = local_down.shape[2]
    factor = 1.0 / math.sqrt(states.shape[0] * data_count * group_count)
    rows = width // (data_count * group_count)
    pieces_down = (
        local_down.reshape(2, group_count, data_count, rows, rank_size)
        .transpose(2, 1, 0, 3, 4)
        .reshape(data_count * group_count, 2, rows, rank_size)
    )
    pieces_up = (
        local_up.reshape(2, rank_size, group_count, data_count, rows)
        .transpose(3, 2, 0, 1, 4)
        .reshape(data_count * group_count, 2, rank_size, rows)
    )
    summed_down, summed_up = (
        lax.psum_scatter(pieces_down, ("dp", "fsdp"), scatter_dimension=0, tiled=True),
        lax.psum_scatter(pieces_up, ("dp", "fsdp"), scatter_dimension=0, tiled=True),
    )
    joined_down, joined_up = (
        lax.all_gather(summed_down, "dp", axis=0, tiled=True),
        lax.all_gather(summed_up, "dp", axis=0, tiled=True),
    )
    shard_down = joined_down.transpose(1, 0, 2, 3).reshape(2, data_count * rows, rank_size)
    shard_up = joined_up.transpose(1, 2, 0, 3).reshape(2, rank_size, data_count * rows)
    return (shard_down * factor, shard_up * factor)


def solution(mesh):
    in_specs = (
        P(("dp", "fsdp"), None),
        P(("dp", "fsdp")),
        P(("dp", "fsdp"), None),
        P(("dp", "fsdp"), None),
        P(("dp", "fsdp"), None),
        P(("dp", "fsdp"), None),
        P(None, "fsdp", None),
        P(None, None, "fsdp"),
    )
    out_specs = (P(None, "fsdp", None), P(None, None, "fsdp"))
    return jax.shard_map(local, mesh=mesh, in_specs=in_specs, out_specs=out_specs, check_vma=False)
```

profile of v0, /device:TPU:1, one launch (start us, length us, event | category | flops | bytes accessed | tf_op | source)
XLA Modules:
  0.0 570.8 jit_solution(748312822632556784)
XLA Ops:
  8.7 2.0 convert_reduce_fusion
  10.8 2.2 fusion.19
  13.0 1.9 fusion.20
  15.6 39.7 %all-gather.3.cloned.1.call-done = bf16[2,5120,128]{2,1,0:T(8,128)(2,1)} async-done(((bf16[2,640,128]{2,1,0:T(8,128)(2,1)}), bf16[2,5120,128]{2,1,0:T(8,128)(2,1)}) %all-gather.3.cloned.1.call-update) | async-done | bytes 2621456 | tf_op jit(solution)/shard_map/all_gather | solution.py:61
  55.2 3.0 fusion.54
  58.3 43.5 %all-gather.5.cloned.1.call-done = bf16[2,128,5120]{2,1,0:T(8,128)(2,1)} async-done(((bf16[2,128,640]{2,1,0:T(8,128)(2,1)}), bf16[2,128,5120]{2,1,0:T(8,128)(2,1)}) %all-gather.5.cloned.1.call-update) | async-done | bytes 2621456 | tf_op jit(solution)/shard_map/all_gather | solution.py:62
  101.8 3.1 fusion.63
  104.9 1.2 fusion.24
  106.1 1.2 fusion.37
  107.3 6.3 %fusion.62 = (f32[40,192]{1,0:T(8,128)S(1)}, f32[40,192,192]{1,2,0:T(8,128)S(1)}) fusion(f32[40,192,192]{1,2,0:T(8,128)S(1)} %fusion.37), kind=kOutput, calls=%fused_computation.77 | output fusion | flops 5898431 | bytes 11827200 | tf_op jit(solution)/shard_map/jvp()/sub | solution.py:45
  113.7 3.6 fusion.33
  117.3 2.9 divide_convert_fusion
  120.2 11.1 %convert_bitcast_fusion = bf16[40,24,8,128]{3,2,1,0:T(8,128)(2,1)} fusion(f32[40,192,192]{1,2,0:T(8,128)S(1)} %get-tuple-element.13, bf16[40,192,192]{1,2,0:T(8,128)(2,1)} %copy-done.3, f32[40,192]{1,0:T(8,128)S(1)} %neg.6, f32[40,192]{1,0:T(8,128)S(1)} %get-tuple-element.12, bf16[192,5120]{1,0:T(8,128)(2,1)S(1)} %copy-done), kind=kOutput, calls=%fused_computation.58 | convolution fusion | flops 2273280000 | bytes 12840960 | tf_op jit(solution)/shard_map/transpose(jvp(qhe,khe->hqk))/dot_general | solution.py:42
  131.3 2.2 copy.93
  133.5 3.6 convert_bitcast_fusion.1
  137.1 0.9 copy.94
  138.0 1.3 copy-done.4
  139.3 5.6 fusion.8
  144.9 8.7 %copy.46 = f32[2,128,5120]{1,0,2:T(2,128)} copy(f32[2,128,5120]{2,1,0:T(8,128)} %fusion.8) | data formatting | bytes 10485760 | tf_op jit(solution)/shard_map/transpose(jvp(jtr,jrd->jtd))/dot_general | solution.py:34
  153.6 5.5 copy.91
  159.2 6.3 %copy.48 = f32[256,2,128,20]{2,1,3,0:T(2,128)} copy(f32[256,2,128,20]{2,0,3,1:T(8,128)S(1)} %bitcast.118) | data formatting | bytes 10485760 | tf_op jit(solution)/shard_map/reshape | solution.py:90
  165.5 3.6 fusion.53
  169.1 3.2 convolution_bitcast_fusion
  172.3 8.8 %copy.43 = f32[2,5120,128]{2,0,1:T(2,128)} copy(f32[2,5120,128]{1,2,0:T(8,128)} %convolution_bitcast_fusion) | data formatting | bytes 10485760 | tf_op jit(solution)/shard_map/transpose(jvp(td,jdr->jtr))/transpose | solution.py:33
  181.2 5.5 copy.92
  186.7 6.3 %copy.45 = f32[256,2,20,128]{3,1,2,0:T(2,128)} copy(f32[256,2,20,128]{3,0,2,1:T(8,128)S(1)} %bitcast.120) | data formatting | bytes 10485760 | tf_op jit(solution)/shard_map/reshape | solution.py:85
  193.0 285.5 %all-reduce.7.cloned.1.call-done = (f32[256,2,20,128]{3,1,2,0:T(2,128)}, f32[256,2,128,20]{2,1,3,0:T(2,128)}) async-done(((f32[256,2,20,128]{3,1,2,0:T(2,128)}, f32[256,2,128,20]{2,1,3,0:T(2,128)}), (f32[256,2,20,128]{3,1,2,0:T(2,128)}, f32[256,2,128,20]{2,1,3,0:T(2,128)})) %all-reduce.7.cloned.1.call-update) | async-done | bytes 10485776
  478.5 0.7 constant_dynamic-slice_fusion.1
  479.2 42.7 %all_gather.14 = f32[32,2,20,128]{3,1,2,0:T(2,128)S(1)} all-gather(f32[1,2,20,128]{3,1,2,0:T(2,128)S(1)} %constant_dynamic-slice_fusion.1), channel_id=1, replica_groups=mesh['dp'=32,'fsdp'=8] {'dp'}, dimensions={0}, use_global_device_ids=true | all-gather | bytes 675840 | tf_op jit(solution)/shard_map/all_gather | solution.py:97
  522.3 0.9 copy.49
  523.9 38.5 %all_gather.15 = f32[32,2,128,20]{2,1,3,0:T(2,128)S(1)} all-gather(f32[1,2,128,20]{2,1,3,0:T(2,128)S(1)} %constant_dynamic-slice_fusion), channel_id=1, replica_groups=mesh['dp'=32,'fsdp'=8] {'dp'}, dimensions={0}, use_global_device_ids=true | all-gather | bytes 675840 | tf_op jit(solution)/shard_map/all_gather | solution.py:98
  562.7 1.4 copy.50
  (36 shorter events, 3.0 us)
Async XLA Ops:
  7.2 98.9 %copy-start = (bf16[192,5120]{1,0:T(8,128)(2,1)S(1)}, bf16[192,5120]{1,0:T(8,128)(2,1)}, u32[]{:S(2)}) copy-start(bf16[192,5120]{1,0:T(8,128)(2,1)} %param.11) | copy-start | bytes 5898244
  7.2 48.1 %all-gather.3.cloned.1.call-start = ((), (), s32[]{:S(2)}) async-start(), calls=%async_computation | async-start | bytes 2949120 | tf_op jit(solution)/shard_map/all_gather | solution.py:61
  7.9 93.9 %all-gather.5.cloned.1.call-start = ((), (), s32[]{:S(2)}) async-start(), calls=%async_computation.1 | async-start | bytes 2949120 | tf_op jit(solution)/shard_map/all_gather | solution.py:62
  8.7 469.9 %all-reduce.7.cloned.1.call-start = ((), (), s32[]{:S(2)}) async-start(), calls=%async_computation.2 | async-start | bytes 20971520
  8.7 4.3 copy-start.2
  101.8 3.1 copy-start.10
  101.8 3.1 copy-start.11
  107.3 6.3 %copy-start.7 = (bf16[192,5120]{1,0:T(8,128)(2,1)S(1)}, bf16[192,5120]{1,0:T(8,128)(2,1)}, u32[]{:S(2)}) copy-start(bf16[192,5120]{1,0:T(8,128)(2,1)} %param.13) | copy-start | bytes 5898244
  117.3 2.9 copy-start.3
  131.3 2.2 copy-start.8
  138.0 1.3 copy-start.4
  159.1 6.4 %copy-start.5 = (bf16[40,24,8,128]{3,2,0,1:T(8,128)(2,1)S(1)}, bf16[40,24,8,128]{3,2,0,1:T(8,128)(2,1)}, u32[]{:S(2)}) copy-start(bf16[40,24,8,128]{3,2,0,1:T(8,128)(2,1)} %copy-done.4) | copy-start | bytes 5898244
  159.1 6.4 %copy-start.9 = (bf16[2,128,5120]{2,1,0:T(8,128)(2,1)S(1)}, bf16[2,128,5120]{2,1,0:T(8,128)(2,1)}, u32[]{:S(2)}) copy-start(bf16[2,128,5120]{2,1,0:T(8,128)(2,1)} %all-gather.5.cloned.1.call-done) | copy-start | bytes 7864324
  165.5 3.6 copy-start.6
  193.0 371.0 %copy-start.1 = (bf16[192,5120]{1,0:T(8,128)(2,1)S(1)}, bf16[192,5120]{1,0:T(8,128)(2,1)}, u32[]{:S(2)}) copy-start(bf16[192,5120]{1,0:T(8,128)(2,1)} %param.11) | copy-start | bytes 5898244
Sparse Core Ops, SparseCore 0:
  9.8 45.3 all-gather.2
  57.0 44.7 all-gather.4
  193.1 285.3 all-reduce.6
where the time goes:
time: 578 us; the launch traced here: 571 us
  waiting for transfers between devices  370 us (64%)
  blocking collectives  81.1 us (14%)
  local copies, waits for them, and re-layouts  49.4 us (9%)
  matrix products  37.9 us (7%)
  other arithmetic  17.3 us (3%)
  between operations  14.8 us (3%)
    unnamed x4, waiting for transfers between devices  287 us
    all_gather x1, waiting for transfers between devices, local(): lax.all_gather(adapter_up_maps, 'fsdp', axis=2, tiled=True)  43.5 us
    all_gather x1, blocking collectives, local(): lax.all_gather(summed_down, 'dp', axis=0, tiled=True)  42.7 us
    all_gather x1, waiting for transfers between devices, local(): lax.all_gather(adapter_down_maps, 'fsdp', axis=1, tiled=True)  39.7 us
    all_gather x1, blocking collectives, local(): lax.all_gather(summed_up, 'dp', axis=0, tiled=True)  38.5 us
    dot_general x3, matrix products, clip_objective(): delta = jnp.einsum('jtr,jrd->jtd', low, up_matrix, precision=highest)  12.3 us
    dot_general x2, matrix products, clip_objective(): jnp.einsum('qhe,khe->hqk', query, keys, precision=highest)  12.3 us
  transfers between devices with their start and end apart: 3, of which 3 were waited for; matrix products, arithmetic and copies ran while one was open for 2% of the time, Pallas kernels for 0%

commit v1 on v0

--- a/solution.py
+++ b/solution.py
@@ -94,7 +94,9 @@
         lax.psum_scatter(pieces_up, ("dp", "fsdp"), scatter_dimension=0, tiled=True),
     )
     joined_down, joined_up = (
-        lax.all_gather(summed_down, "dp", axis=0, tiled=True),
+        jnp.concatenate(
+            lax.all_to_all(jnp.stack([summed_down] * lax.axis_size("dp")), "dp", 0, 0), axis=0
+        ),
         lax.all_gather(summed_up, "dp", axis=0, tiled=True),
     )
     shard_down = joined_down.transpose(1, 0, 2, 3).reshape(2, data_count * rows, rank_size)

time: 578 us -> 561 us (0.971)
  blocking collectives: 81.1 us -> 51.7 us
  starting transfers between devices: 0.11 us -> 11 us
    all_gather x1 -> x0, blocking collectives: 42.7 us -> none  [local(): lax.all_gather(summed_down, 'dp', axis=0, tiled=True)]
    all_gather x1, blocking collectives: 38.5 us -> 51.7 us  [local(): lax.all_gather(summed_up, 'dp', axis=0, tiled=True)]
    all_to_all x0 -> x1, starting transfers between devices: none -> 10.9 us  [local(): lax.all_to_all(jnp.stack([summed_down] * lax.axis_size('dp')), 'dp', 0, 0)]
  transfers between devices with their start and end apart: 3 -> 4, of which waited for: 3 -> 3; matrix products, arithmetic and copies ran while one was open for 2% -> 2% of each run, Pallas kernels for 0% -> 0%
where the time goes in v1:
time: 561 us; the launch traced here: 554 us
  waiting for transfers between devices  370 us (66%)
  blocking collectives  51.7 us (9%)
  local copies, waits for them, and re-layouts  50.6 us (9%)
  matrix products  37.9 us (7%)
  other arithmetic  17.3 us (3%)
  between operations  14.8 us (3%)
  starting transfers between devices  11 us (2%)
    unnamed x4, waiting for transfers between devices  287 us
    all_gather x1, blocking collectives, local(): lax.all_gather(summed_up, 'dp', axis=0, tiled=True)  51.7 us
    all_gather x1, waiting for transfers between devices, local(): lax.all_gather(adapter_up_maps, 'fsdp', axis=2, tiled=True)  43.5 us
    all_gather x1, waiting for transfers between devices, local(): lax.all_gather(adapter_down_maps, 'fsdp', axis=1, tiled=True)  39.7 us
    dot_general x2, matrix products, clip_objective(): jnp.einsum('qhe,khe->hqk', query, keys, precision=highest)  12.3 us
    dot_general x3, matrix products, clip_objective(): delta = jnp.einsum('jtr,jrd->jtd', low, up_matrix, precision=highest)  12.3 us
  transfers between devices with their start and end apart: 4, of which 3 were waited for; matrix products, arithmetic and copies ran while one was open for 2% of the time, Pallas kernels for 0%

profile of v1, /device:TPU:1, one launch (start us, length us, event | category | flops | bytes accessed | tf_op | source)
XLA Modules:
  0.0 553.5 jit_solution(2721909570493853553)
XLA Ops:
  8.7 2.0 convert_reduce_fusion
  10.8 2.2 fusion.19
  13.0 1.9 fusion.20
  15.6 39.7 %all-gather.3.cloned.1.call-done = bf16[2,5120,128]{2,1,0:T(8,128)(2,1)} async-done(((bf16[2,640,128]{2,1,0:T(8,128)(2,1)}), bf16[2,5120,128]{2,1,0:T(8,128)(2,1)}) %all-gather.3.cloned.1.call-update) | async-done | bytes 2621456 | tf_op jit(solution)/shard_map/all_gather | solution.py:61
  55.2 3.0 fusion.54
  58.3 43.5 %all-gather.5.cloned.1.call-done = bf16[2,128,5120]{2,1,0:T(8,128)(2,1)} async-done(((bf16[2,128,640]{2,1,0:T(8,128)(2,1)}), bf16[2,128,5120]{2,1,0:T(8,128)(2,1)}) %all-gather.5.cloned.1.call-update) | async-done | bytes 2621456 | tf_op jit(solution)/shard_map/all_gather | solution.py:62
  101.8 3.1 fusion.63
  104.9 1.2 fusion.24
  106.1 1.2 fusion.37
  107.3 6.3 %fusion.62 = (f32[40,192]{1,0:T(8,128)S(1)}, f32[40,192,192]{1,2,0:T(8,128)S(1)}) fusion(f32[40,192,192]{1,2,0:T(8,128)S(1)} %fusion.37), kind=kOutput, calls=%fused_computation.77 | output fusion | flops 5898431 | bytes 11827200 | tf_op jit(solution)/shard_map/jvp()/sub | solution.py:45
  113.7 3.6 fusion.33
  117.3 2.9 divide_convert_fusion
  120.2 11.1 %convert_bitcast_fusion = bf16[40,24,8,128]{3,2,1,0:T(8,128)(2,1)} fusion(f32[40,192,192]{1,2,0:T(8,128)S(1)} %get-tuple-element.15, bf16[40,192,192]{1,2,0:T(8,128)(2,1)} %copy-done.3, f32[40,192]{1,0:T(8,128)S(1)} %neg.6, f32[40,192]{1,0:T(8,128)S(1)} %get-tuple-element.14, bf16[192,5120]{1,0:T(8,128)(2,1)S(1)} %copy-done), kind=kOutput, calls=%fused_computation.58 | convolution fusion | flops 2273280000 | bytes 12840960 | tf_op jit(solution)/shard_map/transpose(jvp(qhe,khe->hqk))/dot_general | solution.py:42
  131.3 2.2 copy.110
  133.5 3.6 convert_bitcast_fusion.1
  137.1 0.9 copy.111
  138.0 1.3 copy-done.4
  139.3 5.6 %fusion.8 = f32[2,128,5120]{2,1,0:T(8,128)} fusion(bf16[2,192,128]{2,1,0:T(8,128)(2,1)S(1)} %fusion.54, bf16[1,192,5120]{2,1,0:T(8,128)(2,1)S(1)} %bitcast.125, bf16[1,192,5120]{2,1,0:T(8,128)(2,1)S(1)} %bitcast.127), kind=kOutput, calls=%fused_computation.12 | convolution fusion | flops 3025797120 | bytes 9273344 | tf_op jit(solution)/shard_map/transpose(jvp(jtr,jrd->jtd))/dot_general | solution.py:34
  144.9 8.7 %copy.63 = f32[2,128,5120]{1,0,2:T(2,128)} copy(f32[2,128,5120]{2,1,0:T(8,128)} %fusion.8) | data formatting | bytes 10485760 | tf_op jit(solution)/shard_map/transpose(jvp(jtr,jrd->jtd))/dot_general | solution.py:34
  153.6 5.5 copy.108
  159.2 6.3 %copy.65 = f32[256,2,128,20]{2,1,3,0:T(2,128)} copy(f32[256,2,128,20]{2,0,3,1:T(8,128)S(1)} %bitcast.122) | data formatting | bytes 10485760 | tf_op jit(solution)/shard_map/reshape | solution.py:90
  165.5 3.6 fusion.53
  169.1 3.2 convolution_bitcast_fusion
  172.3 8.8 %copy.60 = f32[2,5120,128]{2,0,1:T(2,128)} copy(f32[2,5120,128]{1,2,0:T(8,128)} %convolution_bitcast_fusion) | data formatting | bytes 10485760 | tf_op jit(solution)/shard_map/transpose(jvp(td,jdr->jtr))/transpose | solution.py:33
  181.2 5.5 copy.109
  186.7 6.3 %copy.62 = f32[256,2,20,128]{3,1,2,0:T(2,128)} copy(f32[256,2,20,128]{3,0,2,1:T(8,128)S(1)} %bitcast.124) | data formatting | bytes 10485760 | tf_op jit(solution)/shard_map/reshape | solution.py:85
  193.0 285.7 %all-reduce.7.cloned.1.call-done = (f32[256,2,20,128]{3,1,2,0:T(2,128)}, f32[256,2,128,20]{2,1,3,0:T(2,128)}) async-done(((f32[256,2,20,128]{3,1,2,0:T(2,128)}, f32[256,2,128,20]{2,1,3,0:T(2,128)}), (f32[256,2,20,128]{3,1,2,0:T(2,128)}, f32[256,2,128,20]{2,1,3,0:T(2,128)})) %all-reduce.7.cloned.1.call-update) | async-done | bytes 10485776
  479.6 1.0 stack.2
  480.6 10.9 %all-to-all-start = ((f32[32,1,2,20,128]{4,2,3,1,0:T(2,128)}), f32[32,1,2,20,128]{4,2,3,1,0:T(2,128)S(1)}, u32[]{:S(2)}, u32[]{:S(2)}) async-start(f32[32,1,2,20,128]{4,2,3,1,0:T(2,128)} %stack.2), calls=%async_computation | async-start | bytes 1310720 | tf_op jit(solution)/shard_map/all_to_all | solution.py:98
  492.2 51.7 %all_gather.11 = f32[32,2,128,20]{2,1,3,0:T(2,128)S(1)} all-gather(f32[1,2,128,20]{2,1,3,0:T(2,128)S(1)} %constant_dynamic-slice_fusion), channel_id=1, replica_groups=mesh['dp'=32,'fsdp'=8] {'dp'}, dimensions={0}, use_global_device_ids=true | all-gather | bytes 675840 | tf_op jit(solution)/shard_map/all_gather | solution.py:100
  544.2 1.4 copy.67
  545.9 0.9 copy.66
  (38 shorter events, 3.9 us)
Async XLA Ops:
  7.2 98.9 %copy-start = (bf16[192,5120]{1,0:T(8,128)(2,1)S(1)}, bf16[192,5120]{1,0:T(8,128)(2,1)}, u32[]{:S(2)}) copy-start(bf16[192,5120]{1,0:T(8,128)(2,1)} %param.11) | copy-start | bytes 5898244
  7.2 48.1 %all-gather.3.cloned.1.call-start = ((), (), s32[]{:S(2)}) async-start(), calls=%async_computation.1 | async-start | bytes 2949120 | tf_op jit(solution)/shard_map/all_gather | solution.py:61
  7.9 93.9 %all-gather.5.cloned.1.call-start = ((), (), s32[]{:S(2)}) async-start(), calls=%async_computation.2 | async-start | bytes 2949120 | tf_op jit(solution)/shard_map/all_gather | solution.py:62
  8.7 470.0 %all-reduce.7.cloned.1.call-start = ((), (), s32[]{:S(2)}) async-start(), calls=%async_computation.3 | async-start | bytes 20971520
  8.7 4.3 copy-start.2
  101.8 3.1 copy-start.10
  101.8 3.1 copy-start.11
  107.3 6.3 %copy-start.7 = (bf16[192,5120]{1,0:T(8,128)(2,1)S(1)}, bf16[192,5120]{1,0:T(8,128)(2,1)}, u32[]{:S(2)}) copy-start(bf16[192,5120]{1,0:T(8,128)(2,1)} %param.13) | copy-start | bytes 5898244
  117.3 2.9 copy-start.3
  131.3 2.2 copy-start.8
  138.0 1.3 copy-start.4
  159.1 6.4 %copy-start.5 = (bf16[40,24,8,128]{3,2,0,1:T(8,128)(2,1)S(1)}, bf16[40,24,8,128]{3,2,0,1:T(8,128)(2,1)}, u32[]{:S(2)}) copy-start(bf16[40,24,8,128]{3,2,0,1:T(8,128)(2,1)} %copy-done.4) | copy-start | bytes 5898244
  159.2 6.4 %copy-start.9 = (bf16[2,128,5120]{2,1,0:T(8,128)(2,1)S(1)}, bf16[2,128,5120]{2,1,0:T(8,128)(2,1)}, u32[]{:S(2)}) copy-start(bf16[2,128,5120]{2,1,0:T(8,128)(2,1)} %all-gather.5.cloned.1.call-done) | copy-start | bytes 7864324
  165.5 3.6 copy-start.6
  478.7 68.1 %copy-start.1 = (bf16[192,5120]{1,0:T(8,128)(2,1)S(1)}, bf16[192,5120]{1,0:T(8,128)(2,1)}, u32[]{:S(2)}) copy-start(bf16[192,5120]{1,0:T(8,128)(2,1)} %param.11) | copy-start | bytes 5898244
  480.6 65.0 %all-to-all-start = ((f32[32,1,2,20,128]{4,2,3,1,0:T(2,128)}), f32[32,1,2,20,128]{4,2,3,1,0:T(2,128)S(1)}, u32[]{:S(2)}, u32[]{:S(2)}) async-start(f32[32,1,2,20,128]{4,2,3,1,0:T(2,128)} %stack.2), calls=%async_computation | async-start | bytes 1310720 | tf_op jit(solution)/shard_map/all_to_all | solution.py:98
Sparse Core Ops, SparseCore 0:
  9.8 45.3 all-gather.2
  57.0 44.7 all-gather.4
  193.1 285.5 all-reduce.6
